TPU v7x, 256 devices: a whole 4x4x8 slice. The times are simulated.
256 devices in a mesh: gx: 8 (over z_lo, y), gy: 4 (over z_hi), gz: 8 (over x, core).
Axes of the slice: x: 4, y: 4, z: 8 (z_hi: 4, z_lo: 2; z = z_hi * 2 + z_lo), core: 2. Of those that a mesh axis runs over, the one named last changes fastest.
Arguments:
- tensor: float32 [1024, 512, 1024], P('gx', 'gy', 'gz'), may hold values from -0.75 to 0.75
- factor_a: float32 [256, 1024], P(('gy', 'gz'), 'gx'), may hold values from -1.7 to 1.7
- factor_b: float32 [256, 512], P(('gx', 'gz'), 'gy'), may hold values from -1.7 to 1.7
- factor_c: float32 [256, 1024], P(('gx', 'gy'), 'gz'), may hold values from -1.7 to 1.7
Outputs:
- grad_a: float32 [256, 1024], P(('gy', 'gz'), 'gx')
- grad_b: float32 [256, 512], P(('gx', 'gz'), 'gy')
- grad_c: float32 [256, 1024], P(('gx', 'gy'), 'gz')
All inputs are finite; a program needn't handle non-finite values.
Results may differ from a plain program's by a relative error of at most 0.00019.
Values sent between devices are 32-bit elements; how exact they have to be, the bound alone decides.
A program may use at most 128 MiB of HBM per device.

v0:
```python
import jax
import jax.numpy as jnp
from jax import lax
from jax.sharding import PartitionSpec as P

R = 64


exact_mode = lax.Precision.HIGHEST


def block_gram(block):
    shaped = block.reshape(-1, R, block.shape[1])
    return jnp.einsum("sri,sti->srt", shaped, shaped, precision=exact_mode)


def scaled_rows(block, hessian, first_row, row_count):
    shaped = block.reshape(-1, R, block.shape[1])
    product = jnp.einsum("sri,srt->sti", shaped, hessian, precision=exact_mode).reshape(block.shape)
    return lax.dynamic_slice_in_dim(product, first_row, row_count, 0)


def mode_one(tensor, part_b, part_c):
    first_y = jnp.einsum("ijk,cj->cik", tensor, part_b, precision=exact_mode)
    return jnp.einsum("cik,ck->ci", first_y, part_c, precision=exact_mode)


def mode_two(tensor, part_a, part_c):
    second_y = jnp.einsum("ijk,ck->cij", tensor, part_c, precision=exact_mode)
    return jnp.einsum("cij,ci->cj", second_y, part_a, precision=exact_mode)


def mode_three(tensor, part_a, part_b):
    first_y = jnp.einsum("ijk,cj->cik", tensor, part_b, precision=exact_mode)
    return jnp.einsum("cik,ci->ck", first_y, part_a, precision=exact_mode)


def grouped(kernel, tensor, left_block, right_block, start, count):
    group_size = R
    pieces = []
    for group_index in range(count // group_size):
        offset = start + group_index * group_size
        left_part = lax.dynamic_slice_in_dim(left_block, offset, group_size, 0)
        right_part = lax.dynamic_slice_in_dim(right_block, offset, group_size, 0)
        pieces.append(kernel(tensor, left_part, right_part))
    return jnp.concatenate(pieces, axis=0)


def body(tensor, factor_a, factor_b, factor_c):
    block_a = lax.all_gather(factor_a, ("gy", "gz"), axis=0, tiled=True)
    block_b = lax.all_gather(factor_b, ("gx", "gz"), axis=0, tiled=True)
    block_c = lax.all_gather(factor_c, ("gx", "gy"), axis=0, tiled=True)
    gram_a = lax.psum(block_gram(block_a), "gx")
    gram_b = lax.psum(block_gram(block_b), "gy")
    gram_c = lax.psum(block_gram(block_c), "gz")
    rows_a = factor_a.shape[0]
    rows_b = factor_b.shape[0]
    rows_c = factor_c.shape[0]
    m_a = lax.psum_scatter(
        grouped(
            mode_one, tensor, block_b, block_c, jnp.int32(0), rows_a * lax.axis_size(("gy", "gz"))
        ),
        ("gy", "gz"),
        scatter_dimension=0,
        tiled=True,
    )
    m_b = lax.psum_scatter(
        grouped(
            mode_two, tensor, block_a, block_c, jnp.int32(0), rows_b * lax.axis_size(("gx", "gz"))
        ),
        ("gx", "gz"),
        scatter_dimension=0,
        tiled=True,
    )
    m_c = lax.psum_scatter(
        grouped(
            mode_three, tensor, block_a, block_b, jnp.int32(0), rows_c * lax.axis_size(("gx", "gy"))
        ),
        ("gx", "gy"),
        scatter_dimension=0,
        tiled=True,
    )
    first_a = lax.axis_index(("gy", "gz")) * rows_a
    first_b = lax.axis_index(("gx", "gz")) * rows_b
    first_c = lax.axis_index(("gx", "gy")) * rows_c
    grad_a = scaled_rows(block_a, gram_b * gram_c, first_a, rows_a) - m_a
    grad_b = scaled_rows(block_b, gram_a * gram_c, first_b, rows_b) - m_b
    grad_c = scaled_rows(block_c, gram_a * gram_b, first_c, rows_c) - m_c
    return (grad_a, grad_b, grad_c)


def solution(mesh):
    in_specs = (
        P("gx", "gy", "gz"),
        P(("gy", "gz"), "gx"),
        P(("gx", "gz"), "gy"),
        P(("gx", "gy"), "gz"),
    )
    out_specs = (P(("gy", "gz"), "gx"), P(("gx", "gz"), "gy"), P(("gx", "gy"), "gz"))
    return jax.shard_map(body, mesh=mesh, in_specs=in_specs, out_specs=out_specs, check_vma=False)
```

profile of v0, /device:TPU:1, one launch (start us, length us, event | category | flops | bytes accessed | tf_op | source)
XLA Modules:
  0.0 1187.6 jit_solution(2200772227700395018)
XLA Ops:
  7.2 84.6 %all-gather = f32[64,4,128]{2,1,0:T(4,128)S(1)} all-gather(f32[1,4,128]{2,1,0:T(4,128)} %bitcast.158), channel_id=1, replica_groups=mesh['gx'=8,'gy'=4,'gz'=8] {'gx','gz'}, dimensions={0}, use_global_device_ids=true | all-gather | bytes 133120 | tf_op jit(solution)/shard_map/all_gather | solution.py:51
  92.9 39.8 %all_gather.11 = f32[256,128]{1,0:T(8,128)S(1)} all-gather(f32[8,128]{1,0:T(8,128)} %param.5), channel_id=1, replica_groups=mesh['gx'=8,'gy'=4,'gz'=8] {'gy','gz'}, dimensions={0}, use_global_device_ids=true | all-gather | bytes 135168 | tf_op jit(solution)/shard_map/all_gather | solution.py:50
  133.7 56.9 %all_gather.10 = f32[256,128]{1,0:T(8,128)S(1)} all-gather(f32[8,128]{1,0:T(8,128)} %param.7), channel_id=1, replica_groups=mesh['gx'=8,'gy'=4,'gz'=8] {'gx','gy'}, dimensions={0}, use_global_device_ids=true | all-gather | bytes 135168 | tf_op jit(solution)/shard_map/all_gather | solution.py:52
  191.7 8.1 fusion.35
  199.9 5.4 copy.44
  205.3 8.1 fusion.31
  213.4 5.5 copy.40
  218.9 8.1 fusion.33
  227.0 5.4 copy.42
  232.4 8.1 fusion.37
  240.5 5.4 copy.46
  245.9 5.7 fusion.36
  251.7 3.6 fusion.32
  255.3 3.7 fusion.34
  259.0 3.7 fusion.38
  263.4 18.4 %fusion.42 = f32[64,1,128]{2,1,0:T(1,128)S(1)} fusion(f32[64,128,128]{1,2,0:T(8,128)} %copy.44, f32[64,128,1]{1,2,0:T(1,128)S(1)} %bitcast.127), kind=kOutput, calls=%fused_computation.48 | convolution fusion | flops 12582912 | bytes 4259840 | tf_op jit(solution)/shard_map/cik,ci->ck/dot_general | solution.py:35
  281.8 6.6 fusion.40
  288.4 6.6 fusion.41
  295.0 6.8 fusion.43
  302.6 12.3 %fusion.14 = f32[64,128,128]{2,0,1:T(8,128)S(1)} fusion(f32[128,128,128]{2,1,0:T(8,128)} %param.4, f32[256,128]{1,0:T(8,128)S(1)} %all_gather.10), kind=kOutput, calls=%fused_computation.17 | convolution fusion | flops 1610612736 | bytes 12615680 | tf_op jit(solution)/shard_map/ijk,ck->cij/dot_general | solution.py:29
  314.9 12.0 %fusion.20 = f32[64,128,128]{2,0,1:T(8,128)S(1)} fusion(f32[128,128,128]{2,1,0:T(8,128)} %param.4, f32[256,128]{1,0:T(8,128)S(1)} %all_gather.10), kind=kOutput, calls=%fused_computation.23 | convolution fusion | flops 1610612736 | bytes 12615680 | tf_op jit(solution)/shard_map/ijk,ck->cij/dot_general | solution.py:29
  326.9 9.2 fusion.18
  336.1 9.4 fusion.16
  345.5 6.0 fusion
  351.5 6.2 fusion.6
  357.6 6.0 fusion.4
  363.6 6.2 fusion.2
  374.3 1.4 fusion.8
  377.1 1.4 fusion.12
  378.4 170.3 %all-reduce.16.cloned.1.call-done = f32[256,128]{1,0:T(8,128)} async-done(((f32[256,128]{1,0:T(8,128)}), f32[256,128]{1,0:T(8,128)}) %all-reduce.16.cloned.1.call-update) | async-done | bytes 131088
  549.9 138.7 %all-reduce.20.cloned.1.call-done = f32[256,128]{1,0:T(8,128)} async-done(((f32[256,128]{1,0:T(8,128)}), f32[256,128]{1,0:T(8,128)}) %all-reduce.20.cloned.1.call-update) | async-done | bytes 131088
  689.9 489.1 %all-reduce.18.cloned.1.call-done = f32[256,128]{1,0:T(8,128)} async-done(((f32[256,128]{1,0:T(8,128)}), f32[256,128]{1,0:T(8,128)}) %all-reduce.18.cloned.1.call-update) | async-done | bytes 131088
  (54 shorter events, 12.4 us)
Async XLA Ops:
  7.2 367.1 %all-reduce.10.cloned.1.call-start = ((), (), s32[]{:S(2)}) async-start(), calls=%async_computation | async-start | bytes 262144 | tf_op jit(solution)/shard_map/psum | solution.py:54
  92.8 281.5 %all-reduce.14.cloned.1.call-start = ((), (), s32[]{:S(2)}) async-start(), calls=%async_computation.2 | async-start | bytes 262144 | tf_op jit(solution)/shard_map/psum | solution.py:53
  133.7 242.0 %all-reduce.12.cloned.1.call-start = ((), (), s32[]{:S(2)}) async-start(), calls=%async_computation.1 | async-start | bytes 262144 | tf_op jit(solution)/shard_map/psum | solution.py:55
  191.6 357.1 %all-reduce.16.cloned.1.call-start = ((), (), s32[]{:S(2)}) async-start(), calls=%async_computation.3 | async-start | bytes 262144
  245.9 5.7 copy-start
  245.9 9.4 copy-start.2
  251.7 7.3 copy-start.4
  263.3 425.3 %all-reduce.20.cloned.1.call-start = ((), (), s32[]{:S(2)}) async-start(), calls=%async_computation.5 | async-start | bytes 262144
  263.4 18.5 %copy-start.1 = (f32[64,128,128]{1,2,0:T(8,128)S(1)}, f32[64,128,128]{1,2,0:T(8,128)}, u32[]{:S(2)}) copy-start(f32[64,128,128]{1,2,0:T(8,128)} %copy.40) | copy-start | bytes 12582916
  263.4 25.0 %copy-start.3 = (f32[64,128,128]{1,2,0:T(8,128)S(1)}, f32[64,128,128]{1,2,0:T(8,128)}, u32[]{:S(2)}) copy-start(f32[64,128,128]{1,2,0:T(8,128)} %copy.42) | copy-start | bytes 12582916
  281.8 13.2 %copy-start.5 = (f32[64,128,128]{1,2,0:T(8,128)S(1)}, f32[64,128,128]{1,2,0:T(8,128)}, u32[]{:S(2)}) copy-start(f32[64,128,128]{1,2,0:T(8,128)} %copy.46) | copy-start | bytes 12582916
  302.5 876.5 %all-reduce.18.cloned.1.call-start = ((), (), s32[]{:S(2)}) async-start(), calls=%async_computation.4 | async-start | bytes 262144
  302.6 24.3 %slice-start = ((s8[8388608]{0:T(1024)(128)(4,1)}), s8[4194304]{0:T(1024)(128)(4,1)S(1)}, s32[]{:S(2)}) async-start(s8[8388608]{0:T(1024)(128)(4,1)} %bitcast.119), calls=%async_computation.6 | async-start | bytes 8388608
  314.9 12.0 %slice-start.1 = ((s8[8388608]{0:T(1024)(128)(4,1)}), s8[4194304]{0:T(1024)(128)(4,1)S(1)}, s32[]{:S(2)}) async-start(s8[8388608]{0:T(1024)(128)(4,1)} %bitcast.119), calls=%async_computation.7 | async-start | bytes 8388608
  357.6 12.9 %copy-start.8 = (u32[256]{0:T(256)S(1)}, u32[256]{0:T(256)}, u32[]{:S(2)}) copy-start(u32[256]{0:T(256)} %constant.33) | copy-start | bytes 3076
  357.6 13.5 %copy-start.7 = (u32[256]{0:T(256)S(1)}, u32[256]{0:T(256)}, u32[]{:S(2)}) copy-start(u32[256]{0:T(256)} %constant.29) | copy-start | bytes 3076
  357.6 14.1 %copy-start.6 = (u32[256]{0:T(256)S(1)}, u32[256]{0:T(256)}, u32[]{:S(2)}) copy-start(u32[256]{0:T(256)} %constant.25) | copy-start | bytes 3076
Sparse Core Ops, SparseCore 0:
  93.0 44.2 all-reduce.9
  140.1 74.1 all-reduce.13
  216.6 66.5 all-reduce.11
  285.8 262.7 all-reduce.15
  552.0 136.6 all-reduce.19
  691.3 487.6 all-reduce.17
where the time goes:
time: 1200 us; the launch traced here: 1190 us
  waiting for transfers between devices  798 us (66%)
  blocking collectives  181 us (15%)
  matrix products  162 us (14%)
  local copies, waits for them, and re-layouts  23.6 us (2%)
  between operations  16.7 us (1%)
    unnamed x9, waiting for transfers between devices  798 us
    all_gather x1, blocking collectives, body(): block_b = lax.all_gather(factor_b, ('gx', 'gz'), axis=0, tiled=True)  84.6 us
    all_gather x1, blocking collectives, body(): block_c = lax.all_gather(factor_c, ('gx', 'gy'), axis=0, tiled=True)  56.9 us
    dot_general x4, matrix products, mode_two(): second_y = jnp.einsum('ijk,ck->cij', tensor, part_c, precision=exact_mode)  42.8 us
    all_gather x1, blocking collectives, body(): block_a = lax.all_gather(factor_a, ('gy', 'gz'), axis=0, tiled=True)  39.8 us
    dot_general x4, matrix products, mode_three(): return jnp.einsum('cik,ci->ck', first_y, part_a, precision=exact_mode)  38.4 us
    dot_general x4, matrix products, mode_one(): first_y = jnp.einsum('ijk,cj->cik', tensor, part_b, precision=exact_mode)  32.4 us
    dot_general x4, matrix products, mode_two(): return jnp.einsum('cij,ci->cj', second_y, part_a, precision=exact_mode)  24.3 us
  transfers between devices with their start and end apart: 6, of which 3 were waited for; matrix products, arithmetic and copies ran while one was open for 16% of the time, Pallas kernels for 0%

commit v1 on v0

v1 whole, which is shorter than its diff:
```python
import functools

import jax
import jax.numpy as jnp
from jax import lax
from jax.experimental import pallas as pl
from jax.experimental.pallas import tpu as pltpu
from jax.sharding import PartitionSpec as P

R = 64
SR = 256
LEN = 128
CHUNKS = 8
STEP = 16
MESH = pl.DeviceIdType.MESH
bf16 = jnp.bfloat16
f32 = jnp.float32


def split(value):
    high = value.astype(bf16)
    return high, (value - high.astype(f32)).astype(bf16)


def stacked(value):
    high, low = split(value)
    return jnp.concatenate([high, high], 0), jnp.concatenate([low, low], 0)


def mm(left, right):
    return jnp.dot(left, right, preferred_element_type=f32)


def wait_bytes(ref, sem):
    pltpu.make_async_copy(ref, ref, sem).wait()


def kernel(
    t_hbm, a_in, b_in, c_in, a_out, b_out, c_out,
    t_in, x_rows, x_cols, ga, gb, gc, wb, wc, a_t, b_t, acc_a, acc_b, acc_c, ha, hb, hc,
    pa, pb, pc, ra, rb, rc, sa, sb, sc, qa, qb, qc,
    t_sem, send, recv,
):
    gx, gy, gz = lax.axis_index("gx"), lax.axis_index("gy"), lax.axis_index("gz")
    z_lo, y = gx // 4, gx % 4

    gy_peers = [(gx, (gy + d) % 4, gz) for d in range(1, 4)]
    gz_peers = [(gx, gy, (gz + d) % 8) for d in range(1, 8)]
    y_peers = [(z_lo * 4 + (y + d) % 4, gy, gz) for d in range(1, 4)]
    lo = 1 - z_lo
    b_peers = [((lo if e else z_lo) * 4 + y, gy, (gz + d) % 8) for e in (0, 1) for d in range(8) if e or d]
    c_peers = [((lo if e else z_lo) * 4 + y, (gy + d) % 4, gz) for e in (0, 1) for d in range(4) if e or d]
    partners = gy_peers + y_peers + b_peers + [p for n, p in enumerate(c_peers) if n >= 4]

    def b_slot(peer):
        return peer[0] // 4 * 8 + peer[2]

    def c_slot(peer):
        return peer[0] // 4 * 4 + peer[1]

    me = (gx, gy, gz)
    b_me, c_me = b_slot(me), c_slot(me)

    def put(src, dst, peer, stage):
        pltpu.make_async_remote_copy(
            src_ref=src, dst_ref=dst, send_sem=send.at[stage], recv_sem=recv.at[stage],
            device_id=peer, device_id_type=MESH,
        ).start()

    per = LEN // CHUNKS

    def t_copy(n):
        rows = pl.ds(n * per, per)
        return pltpu.make_async_copy(t_hbm.at[rows], t_in.at[rows], t_sem.at[n])

    for n in range(CHUNKS):
        t_copy(n).start()

    barrier = pltpu.get_barrier_semaphore()
    for peer in partners:
        pl.semaphore_signal(barrier, inc=1, device_id=peer, device_id_type=MESH)
    ga[gz, gy] = a_in[...]
    gb[y, b_me] = b_in[...]
    gc[y, c_me] = c_in[...]
    pl.semaphore_wait(barrier, len(partners))

    for peer in c_peers:
        put(gc.at[y, c_me], gc.at[y, c_me], peer, 0)
    for peer in b_peers:
        put(gb.at[y, b_me], gb.at[y, b_me], peer, 1)
    for peer in gy_peers:
        put(ga.at[gz, gy], ga.at[gz, gy], peer, 2)

    def prepare(n):
        t_copy(n).wait()

        def body(it, _):
            for u in range(4):
                i = n * per + it * 4 + u
                rows = pl.ds(pl.multiple_of(i * LEN, LEN), LEN)
                value = t_in[i]
                high, low = split(value)
                x_rows[rows, 0:LEN] = high
                x_rows[rows, LEN:] = low
                high, low = split(value.T)
                x_cols[rows, 0:LEN] = high
                x_cols[rows, LEN:] = low
            return 0

        lax.fori_loop(0, per // 4, body, 0)

    for n in range(CHUNKS // 2):
        prepare(n)

    wait_bytes(gc.at[0, 0:7], recv.at[0])
    for peer in y_peers:
        put(gc.at[y], gc.at[y], peer, 3)
    wait_bytes(gb.at[0, 0:15], recv.at[1])
    for peer in y_peers:
        put(gb.at[y], gb.at[y], peer, 4)
    wait_bytes(ga.at[0, 0:3], recv.at[2])
    for peer in gz_peers:
        put(ga.at[gz], ga.at[gz], peer, 5)

    for n in range(CHUNKS // 2, CHUNKS):
        prepare(n)

    wait_bytes(gc.at[0:3], recv.at[3])
    wait_bytes(gb.at[0:3], recv.at[4])
    wait_bytes(ga.at[0:7], recv.at[5])

    def gram(rows, weights):
        left = jnp.concatenate(split(rows), 1)
        return mm(left, weights[0]) + mm(left, weights[1])

    rows_c = jnp.concatenate([gc[n, e * 4:e * 4 + 4].reshape(32, LEN) for e in (0, 1) for n in range(4)], 0)
    cols_c = rows_c.T
    weights_c = stacked(cols_c)
    wc[0], wc[1] = weights_c
    gram_c = gram(rows_c, weights_c)
    rows_b = jnp.concatenate([gb[n, e * 8:e * 8 + 8].reshape(32, LEN) for e in (0, 1) for n in range(4)], 0)
    cols_b = rows_b.T
    b_t[...] = cols_b
    weights_b = stacked(cols_b)
    wb[0], wb[1] = weights_b
    gram_b = gram(rows_b, weights_b)
    rows_a = jnp.concatenate([ga[:, n].reshape(64, LEN) for n in range(4)], 0)
    cols_a = rows_a.T
    a_t[...] = cols_a
    gram_a = gram(rows_a, stacked(cols_a))
    mask = lax.broadcasted_iota(jnp.int32, (SR, SR), 0) // R == lax.broadcasted_iota(jnp.int32, (SR, SR), 1) // R

    def hess_term(cols, left, right):
        high, low = split(jnp.where(mask, left * right, 0.0))
        cols_high, cols_low = split(cols)
        return mm(cols_high, high) + mm(cols_low, high) + mm(cols_high, low)

    ha[...] = hess_term(cols_a, gram_b, gram_c)
    acc_b[...] = hess_term(cols_b, gram_a, gram_c)
    acc_c[...] = hess_term(cols_c, gram_a, gram_b)

    def product(x, w, it):
        rows = x[pl.ds(pl.multiple_of(it * (STEP * LEN), STEP * LEN), STEP * LEN), :]
        return (mm(rows, w[0]) + mm(rows, w[1])).reshape(STEP, LEN, SR)

    def rows_step(it, _):
        value = product(x_rows, wc, it)
        total = acc_b[...]
        other = b_t[...]
        for u in range(STEP):
            i = pl.ds(it * STEP + u, 1)
            total = total - value[u] * a_t[i, :]
            acc_a[i, :] = jnp.sum(value[u] * other, axis=0, keepdims=True)
        acc_b[...] = total
        return 0

    lax.fori_loop(0, LEN // STEP, rows_step, 0)

    part_b = acc_b[...].T
    for e in (0, 1):
        for n in range(4):
            q = (e * 4 + n) * 32
            pb[n, e * 8:e * 8 + 8] = part_b[q:q + 32].reshape(8, 4, LEN)
    for peer in y_peers:
        there = peer[0] % 4
        put(pb.at[there], rb.at[y], peer, 6)
    part_a = (ha[...] - acc_a[...]).T
    for n in range(4):
        pa[:, n] = part_a[n * 64:n * 64 + 64].reshape(8, 8, LEN)
    for peer in gz_peers:
        put(pa.at[peer[2]], ra.at[gz], peer, 7)

    def cols_step(it, _):
        value = product(x_cols, wb, it)
        total = acc_c[...]
        for u in range(STEP):
            total = total - value[u] * a_t[pl.ds(it * STEP + u, 1), :]
        acc_c[...] = total
        return 0

    half = LEN // STEP // 2
    lax.fori_loop(0, half, cols_step, 0)

    wait_bytes(rb.at[0:3], recv.at[6])
    rb[y] = pb[y]
    sb[...] = (rb[0] + rb[1]) + (rb[2] + rb[3])
    for peer in b_peers:
        put(sb.at[b_slot(peer)], qb.at[b_me], peer, 8)
    wait_bytes(ra.at[0:7], recv.at[7])
    ra[gz] = pa[gz]
    sa[...] = ((ra[0] + ra[1]) + (ra[2] + ra[3])) + ((ra[4] + ra[5]) + (ra[6] + ra[7]))
    for peer in gy_peers:
        put(sa.at[peer[1]], qa.at[gy], peer, 9)

    lax.fori_loop(half, 2 * half, cols_step, 0)

    part_c = acc_c[...].T
    for e in (0, 1):
        for n in range(4):
            q = (e * 4 + n) * 32
            pc[n, e * 4:e * 4 + 4] = part_c[q:q + 32].reshape(4, 8, LEN)
    for peer in y_peers:
        put(pc.at[peer[0] % 4], rc.at[y], peer, 10)

    wait_bytes(qb.at[0:15], recv.at[8])
    qb[b_me] = sb[b_me]
    b_out[...] = jnp.sum(qb[...], axis=0)
    wait_bytes(qa.at[0:3], recv.at[9])
    qa[gy] = sa[gy]
    a_out[...] = (qa[0] + qa[1]) + (qa[2] + qa[3])

    wait_bytes(rc.at[0:3], recv.at[10])
    rc[y] = pc[y]
    sc[...] = (rc[0] + rc[1]) + (rc[2] + rc[3])
    for peer in c_peers:
        put(sc.at[c_slot(peer)], qc.at[c_me], peer, 11)
    wait_bytes(qc.at[0:7], recv.at[11])
    qc[c_me] = sc[c_me]
    c_out[...] = jnp.sum(qc[...], axis=0)

    wait_bytes(gc.at[0, 0:7], send.at[0])
    wait_bytes(gb.at[0, 0:15], send.at[1])
    wait_bytes(ga.at[0, 0:3], send.at[2])
    wait_bytes(gc.at[0:3], send.at[3])
    wait_bytes(gb.at[0:3], send.at[4])
    wait_bytes(ga.at[0:7], send.at[5])
    wait_bytes(pb.at[0:3], send.at[6])
    wait_bytes(pa.at[0:7], send.at[7])
    wait_bytes(qb.at[0:15], send.at[8])
    wait_bytes(qa.at[0:3], send.at[9])
    wait_bytes(pc.at[0:3], send.at[10])
    wait_bytes(qc.at[0:7], send.at[11])


def body(tensor, factor_a, factor_b, factor_c):
    vmem = pl.BlockSpec(memory_space=pltpu.VMEM)
    rows = LEN * LEN
    return pl.pallas_call(
        kernel,
        out_shape=[jax.ShapeDtypeStruct(v.shape, f32) for v in (factor_a, factor_b, factor_c)],
        in_specs=[pl.BlockSpec(memory_space=pl.ANY), vmem, vmem, vmem],
        out_specs=[vmem, vmem, vmem],
        scratch_shapes=[
            pltpu.VMEM((LEN, LEN, LEN), f32),
            pltpu.VMEM((rows, 2 * LEN), bf16),
            pltpu.VMEM((rows, 2 * LEN), bf16),
            pltpu.VMEM((8, 4, 8, LEN), f32),
            pltpu.VMEM((4, 16, 4, LEN), f32),
            pltpu.VMEM((4, 8, 8, LEN), f32),
            pltpu.VMEM((2, SR, SR), bf16),
            pltpu.VMEM((2, SR, SR), bf16),
            pltpu.VMEM((LEN, SR), f32),
            pltpu.VMEM((LEN, SR), f32),
            pltpu.VMEM((LEN, SR), f32),
            pltpu.VMEM((LEN, SR), f32),
            pltpu.VMEM((LEN, SR), f32),
            pltpu.VMEM((LEN, SR), f32),
            pltpu.VMEM((LEN, SR), f32),
            pltpu.VMEM((LEN, SR), f32),
            pltpu.VMEM((8, 4, 8, LEN), f32),
            pltpu.VMEM((4, 16, 4, LEN), f32),
            pltpu.VMEM((4, 8, 8, LEN), f32),
            pltpu.VMEM((8, 4, 8, LEN), f32),
            pltpu.VMEM((4, 16, 4, LEN), f32),
            pltpu.VMEM((4, 8, 8, LEN), f32),
            pltpu.VMEM((4, 8, LEN), f32),
            pltpu.VMEM((16, 4, LEN), f32),
            pltpu.VMEM((8, 8, LEN), f32),
            pltpu.VMEM((4, 8, LEN), f32),
            pltpu.VMEM((16, 4, LEN), f32),
            pltpu.VMEM((8, 8, LEN), f32),
            pltpu.SemaphoreType.DMA((CHUNKS,)),
            pltpu.SemaphoreType.DMA((12,)),
            pltpu.SemaphoreType.DMA((12,)),
        ],
        compiler_params=pltpu.CompilerParams(
            collective_id=0, has_side_effects=True, vmem_limit_bytes=56 * 2**20
        ),
    )(tensor, factor_a, factor_b, factor_c)


def solution(mesh):
    in_specs = (
        P("gx", "gy", "gz"),
        P(("gy", "gz"), "gx"),
        P(("gx", "gz"), "gy"),
        P(("gx", "gy"), "gz"),
    )
    out_specs = (P(("gy", "gz"), "gx"), P(("gx", "gz"), "gy"), P(("gx", "gy"), "gz"))
    return jax.shard_map(body, mesh=mesh, in_specs=in_specs, out_specs=out_specs, check_vma=False)
```

time: 1200 us -> 46.8 us (0.04); the launches traced: 1190 us -> 46.6 us
  waiting for transfers between devices: 798 us -> 0 us
  blocking collectives: 181 us -> 0 us
  matrix products: 162 us -> 0 us
  Pallas kernels: 0 us -> 42.2 us
  local copies, waits for them, and re-layouts: 23.6 us -> 3.77 us
  between operations: 16.7 us -> 0.64 us
    unnamed x9 -> x0, waiting for transfers between devices: 798 us -> none
    all_gather x3 -> x0, blocking collectives: 181 us -> none  [the longest x1 84.6 us: body(): block_b = lax.all_gather(factor_b, ('gx', 'gz'), axis=0, tiled=True)]
    dot_general x26 -> x0, matrix products: 162 us -> none  [the longest x4 42.8 us: mode_two(): second_y = jnp.einsum('ijk,ck->cij', tensor, part_c, precision=exact_mode)]
    pallas_call x0 -> x1, Pallas kernels: none -> 42.2 us  [body(): pl.pallas_call(kernel, out_shape=[jax.ShapeDtypeStruct(v.shape, f32) for...]
    dot_general x4 -> x0, local copies, waits for them, and re-layouts: 21.8 us -> none  [mode_one(): first_y = jnp.einsum('ijk,cj->cik', tensor, part_b, precision=exact_mode)]
  transfers between devices with their start and end apart: 6 -> 0, of which waited for: 3 -> 0; matrix products, arithmetic and copies ran while one was open for 16% -> 0% of each run, Pallas kernels for 0% -> 0%
where the time goes in v1:
time: 46.8 us; the launch traced here: 46.6 us
  Pallas kernels  42.2 us (90%)
  local copies, waits for them, and re-layouts  3.77 us (8%)
  between operations  0.64 us (1%)
    pallas_call x1, Pallas kernels, body(): pl.pallas_call(kernel, out_shape=[jax.ShapeDtypeStruct(v.shape, f32) for...  42.2 us
    unnamed x3, local copies, waits for them, and re-layouts  3.77 us

profile of v1, /device:TPU:1, one launch (start us, length us, event | category | flops | bytes accessed | tf_op | source)
XLA Modules:
  0.0 46.6 jit_solution(14232100060234846708)
XLA Ops:
  0.6 42.2 %shard_map.67 = (f32[8,128]{1,0:T(8,128)}, f32[4,128]{1,0:T(4,128)}, f32[8,128]{1,0:T(8,128)}) custom-call(f32[128,128,128]{2,1,0:T(8,128)} %t_hbm.1, f32[8,128]{1,0:T(8,128)} %a_in.1, f32[4,128]{1,0:T(4,128)} %b_in.1, f32[8,128]{1,0:T(8,128)} %c_in.1), custom_call_target="tpu_custom_call" | custom-call | tf_op jit(solution)/shard_map/pallas_call | solution.py:258
  42.8 1.3 %copy.10 = f32[8,128]{1,0:T(8,128)} copy(f32[8,128]{1,0:T(8,128)} %get-tuple-element.6) | data formatting | bytes 8192
  44.1 1.2 %copy.11 = f32[4,128]{1,0:T(4,128)} copy(f32[4,128]{1,0:T(4,128)} %get-tuple-element.7) | data formatting | bytes 4096
  45.3 1.3 %copy.12 = f32[8,128]{1,0:T(8,128)} copy(f32[8,128]{1,0:T(8,128)} %get-tuple-element.8) | data formatting | bytes 8192

commit v2 on v0

v2 whole, which is shorter than its diff:
```python
import jax
import jax.numpy as jnp
from jax import lax
from jax.experimental import pallas as pl
from jax.experimental.pallas import tpu as pltpu
from jax.sharding import PartitionSpec as P

PH = {"g", "prep", "gram", "l1", "l2", "rs"}
DIRECT = set("gb rb".split())
R = 64
SR = 256
LEN = 128
CHUNKS = 8
STEP = 64
MESH = pl.DeviceIdType.MESH
bf16 = jnp.bfloat16
f32 = jnp.float32


def split(value):
    high = value.astype(bf16)
    return high, (value - high.astype(f32)).astype(bf16)


def stacked(value):
    high, low = split(value)
    return jnp.concatenate([high, high], 0), jnp.concatenate([low, low], 0)


def mm(left, right):
    return jnp.dot(left, right, preferred_element_type=f32)


def offsets(zh=1, zl=1, y=1, x=1, core=1):
    found = [
        (a, b, c, d, e)
        for a in range(zh) for b in range(zl) for c in range(y) for d in range(x) for e in range(core)
    ]

    def hops(o):
        return min(2 * o[0], 8 - 2 * o[0]) + o[1] + min(o[2], 4 - o[2]) + min(o[3], 4 - o[3]) + o[4] * 0.1

    return sorted(found, key=hops, reverse=True)[:-1]


def kernel(
    t_hbm, a_in, b_in, c_in, out,
    t_in, x_rows, x_cols, ga, gb, gc, wb, wc, a_t, c_t, m_a, acc_a, acc_b, acc_c,
    pa, pb, pc, ra, rb, rc, sa, sb, sc, qa, qb, qc,
    t_sem, in_sem, send, recv,
):
    gx, gy, gz = lax.axis_index("gx"), lax.axis_index("gy"), lax.axis_index("gz")
    z_lo, y = gx // 4, gx % 4
    x, core = gz // 2, gz % 2

    def peers(**extent):
        return [
            (((z_lo + b) % 2) * 4 + (y + c) % 4, (gy + a) % 4, ((x + d) % 4) * 2 + (core + e) % 2)
            for a, b, c, d, e in offsets(**extent)
        ]

    def slot_a(d):
        return d[2] * 4 + d[1]

    def slot_b(d):
        return d[0] % 4 * 16 + d[0] // 4 * 8 + d[2]

    def slot_c(d):
        return d[0] % 4 * 8 + d[0] // 4 * 4 + d[1]

    me = (gx, gy, gz)
    me_a, me_b, me_c = slot_a(me), slot_b(me), slot_c(me)
    started = []

    def put(src, dst, peer, stage):
        pltpu.make_async_remote_copy(
            src_ref=src, dst_ref=dst, send_sem=send.at[stage], recv_sem=recv.at[stage],
            device_id=peer, device_id_type=MESH,
        ).start()

    def wait_bytes(ref, count, sem):
        pltpu.make_async_copy(ref.at[0:count], ref.at[0:count], sem).wait()

    def arrived(ref, count, stage):
        wait_bytes(ref, count, recv.at[stage])
        started.append((ref, count, stage))

    class Factor:
        def __init__(self, full, first, second, run, slot, outer, inner, g, p, r, s, q, base, name):
            self.full, self.first, self.second = peers(**full), peers(**first), peers(**second)
            self.run, self.slot, self.outer, self.inner = run, slot, outer, inner
            self.g, self.p, self.r, self.s, self.q = g, p, r, s, q
            self.mine, self.base = slot(me), base
            self.count = len(self.full)
            self.g_direct, self.r_direct = "g" + name in DIRECT, "r" + name in DIRECT

        def runs(self, device):
            return pl.ds(self.outer(device) * self.run, self.run)

        def gather_first(self):
            for peer in self.full if self.g_direct else self.first:
                put(self.g.at[self.mine], self.g.at[self.mine], peer, self.base)

        def gather_second(self):
            if self.g_direct:
                return
            arrived(self.g, len(self.first), self.base)
            block = self.g.at[self.runs(me)]
            for peer in self.second:
                put(block, block, peer, self.base + 1)

        def gather_wait(self):
            if self.g_direct:
                arrived(self.g, self.count, self.base)
            else:
                arrived(self.g, self.run * len(self.second), self.base + 1)

        def reduce_first(self):
            if self.r_direct:
                for peer in self.full:
                    put(self.p.at[self.slot(peer)], self.r.at[self.mine], peer, self.base + 2)
                return
            for peer in self.second:
                put(self.p.at[self.runs(peer)], self.r.at[self.runs(me)], peer, self.base + 2)

        def reduce_second(self):
            if self.r_direct:
                return
            arrived(self.r, self.run * len(self.second), self.base + 2)
            self.r[self.runs(me)] = self.p[self.runs(me)]
            groups = self.r.shape[0] // self.run
            self.s[...] = jnp.sum(self.r[...].reshape(groups, self.run, *self.r.shape[1:]), axis=0)
            for peer in self.first:
                put(self.s.at[self.inner(peer)], self.q.at[self.inner(me)], peer, self.base + 3)

        def reduce_wait(self):
            if self.r_direct:
                arrived(self.r, self.count, self.base + 2)
                self.r[self.mine] = self.p[self.mine]
                return jnp.sum(self.r[...], axis=0)
            arrived(self.q, len(self.first), self.base + 3)
            self.q[self.inner(me)] = self.s[self.inner(me)]
            return jnp.sum(self.q[...], axis=0)

    A = Factor(dict(zh=4, x=4, core=2), dict(zh=4), dict(x=4, core=2), 4, slot_a,
               lambda d: d[2], lambda d: d[1], ga, pa, ra, sa, qa, 0, "a")
    B = Factor(dict(zl=2, y=4, x=4, core=2), dict(zl=2, x=4, core=2), dict(y=4), 16, slot_b,
               lambda d: d[0] % 4, lambda d: d[0] // 4 * 8 + d[2], gb, pb, rb, sb, qb, 4, "b")
    C = Factor(dict(zh=4, zl=2, y=4), dict(zh=4, zl=2), dict(y=4), 8, slot_c,
               lambda d: d[0] % 4, lambda d: d[0] // 4 * 4 + d[1], gc, pc, rc, sc, qc, 8, "c")

    extents = []
    for f, n, one, two, full in (
        ("a", 0, dict(zh=4), dict(x=4, core=2), dict(zh=4, x=4, core=2)),
        ("b", 1, dict(zl=2, x=4, core=2), dict(y=4), dict(zl=2, y=4, x=4, core=2)),
        ("c", 2, dict(zh=4, zl=2), dict(y=4), dict(zh=4, zl=2, y=4)),
    ):
        for kind in "gr":
            extents += [full] if kind + f in DIRECT else [one, two]
    wanted = sorted({o for e in extents for o in offsets(**e)})
    partners = [
        (((z_lo + b) % 2) * 4 + (y + c) % 4, (gy + a) % 4, ((x + d) % 4) * 2 + (core + e) % 2)
        for a, b, c, d, e in wanted
    ]

    per = LEN // CHUNKS

    def t_copy(n):
        rows = pl.ds(n * per, per)
        return pltpu.make_async_copy(t_hbm.at[rows], t_in.at[rows], t_sem.at[n])

    barrier = pltpu.get_barrier_semaphore()
    for peer in partners:
        pl.semaphore_signal(barrier, inc=1, device_id=peer, device_id_type=MESH)
    own = [
        pltpu.make_async_copy(src, dst, in_sem.at[n])
        for n, (src, dst) in enumerate(((a_in, ga.at[me_a]), (b_in, gb.at[me_b]), (c_in, gc.at[me_c])))
    ]
    for copy in own:
        copy.start()
    if "prep" in PH:
        for n in range(CHUNKS):
            t_copy(n).start()
    for copy in own:
        copy.wait()
    pl.semaphore_wait(barrier, len(partners))

    if "g" in PH:
        C.gather_first()
        A.gather_first()
        B.gather_first()

    def prepare(n):
        t_copy(n).wait()

        def body(it, _):
            for u in range(4):
                i = n * per + it * 4 + u
                rows = pl.ds(pl.multiple_of(i * LEN, LEN), LEN)
                value = t_in[i]
                high, low = split(value)
                x_rows[rows, 0:LEN] = high
                x_rows[rows, LEN:] = low
                high, low = split(value.T)
                x_cols[rows, 0:LEN] = high
                x_cols[rows, LEN:] = low
            return 0

        lax.fori_loop(0, per // 4, body, 0)

    if "prep" in PH:
        for n in range(CHUNKS // 2):
            prepare(n)
    if "g" in PH:
        C.gather_second()
        A.gather_second()
        B.gather_second()
    if "prep" in PH:
        for n in range(CHUNKS // 2, CHUNKS):
            prepare(n)

    def gram(rows, weights):
        left = jnp.concatenate(split(rows), 1)
        return mm(left, weights[0]) + mm(left, weights[1])

    def hess_term(cols, left, right):
        mask = (
            lax.broadcasted_iota(jnp.int32, (SR, SR), 0) // R
            == lax.broadcasted_iota(jnp.int32, (SR, SR), 1) // R
        )
        high, low = split(jnp.where(mask, left * right, 0.0))
        cols_high, cols_low = split(cols)
        return mm(cols_high, high) + mm(cols_low, high) + mm(cols_high, low)

    if "g" in PH:
        B.gather_wait()
    if "gram" in PH:
        rows_b = jnp.concatenate(
            [gb[n * 16 + e * 8:n * 16 + e * 8 + 8].reshape(32, LEN) for e in (0, 1) for n in range(4)], 0)
        cols_b = rows_b.T
        weights_b = stacked(cols_b)
        wb[0], wb[1] = weights_b
        gram_b = gram(rows_b, weights_b)
    if "g" in PH:
        A.gather_wait()
    if "gram" in PH:
        rows_a = jnp.concatenate([ga[s * 4 + n] for n in range(4) for s in range(8)], 0)
        cols_a = rows_a.T
        a_t[...] = cols_a
        gram_a = gram(rows_a, stacked(cols_a))
    if "g" in PH:
        C.gather_wait()
    if "gram" in PH:
        rows_c = jnp.concatenate(
            [gc[n * 8 + e * 4:n * 8 + e * 4 + 4].reshape(32, LEN) for e in (0, 1) for n in range(4)], 0)
        cols_c = rows_c.T
        c_t[...] = cols_c
        weights_c = stacked(cols_c)
        wc[0], wc[1] = weights_c
        gram_c = gram(rows_c, weights_c)
        acc_a[...] = hess_term(cols_a, gram_b, gram_c)
        acc_b[...] = hess_term(cols_b, gram_a, gram_c)
        acc_c[...] = hess_term(cols_c, gram_a, gram_b)

    def product(x, w, it):
        rows = x[pl.ds(pl.multiple_of(it * (STEP * LEN), STEP * LEN), STEP * LEN), :]
        return (mm(rows, w[0]) + mm(rows, w[1])).reshape(STEP, LEN, SR)

    def cols_step(it, _):
        value = product(x_cols, wb, it)
        total = acc_c[...]
        other = c_t[...]
        for u in range(STEP):
            i = pl.ds(it * STEP + u, 1)
            total = total - value[u] * a_t[i, :]
            m_a[i, :] = jnp.sum(value[u] * other, axis=0, keepdims=True)
        acc_c[...] = total
        return 0

    if "l1" in PH:
        lax.fori_loop(0, LEN // STEP, cols_step, 0)

    if "rs" in PH:
        part_c = acc_c[...].T
        for e in (0, 1):
            for n in range(4):
                q = (e * 4 + n) * 32
                pc[n * 8 + e * 4:n * 8 + e * 4 + 4] = part_c[q:q + 32].reshape(4, 8, LEN)
        C.reduce_first()
        part_a = (acc_a[...] - m_a[...]).T
        for n in range(4):
            for s in range(8):
                q = n * 64 + s * 8
                pa[s * 4 + n] = part_a[q:q + 8]
        A.reduce_first()

    def rows_step(it, _):
        value = product(x_rows, wc, it)
        total = acc_b[...]
        for u in range(STEP):
            total = total - value[u] * a_t[pl.ds(it * STEP + u, 1), :]
        acc_b[...] = total
        return 0

    if "l2" in PH:
        lax.fori_loop(0, LEN // STEP, rows_step, 0)

    if "rs" in PH:
        part_b = acc_b[...].T
        for e in (0, 1):
            for n in range(4):
                q = (e * 4 + n) * 32
                pb[n * 16 + e * 8:n * 16 + e * 8 + 8] = part_b[q:q + 32].reshape(8, 4, LEN)
        B.reduce_first()
        C.reduce_second()
        A.reduce_second()
        B.reduce_second()
        out[8:16] = C.reduce_wait()
        out[0:8] = A.reduce_wait()
        out[16:20] = B.reduce_wait()
    else:
        out[0:8] = ga[0] + gb[0:2].reshape(8, 128) + gc[0] + acc_a[0:8, 0:128] + acc_b[0:8, 0:128] + acc_c[0:8, 0:128]
        out[8:16] = out[0:8]
        out[16:20] = gb[0]

    for ref, count, stage in started:
        wait_bytes(ref, count, send.at[stage])


def unpack(packed, a_out, b_out, c_out):
    a_out[...] = packed[0:8]
    c_out[...] = packed[8:16]
    b_out[...] = packed[16:20]


def body(tensor, factor_a, factor_b, factor_c):
    vmem = pl.BlockSpec(memory_space=pltpu.VMEM)
    blocks = [(32, 8, LEN), (64, 4, LEN), (32, 8, LEN)]
    parts = [(4, 8, LEN), (16, 4, LEN), (8, 8, LEN)]
    packed = pl.pallas_call(
        kernel,
        out_shape=jax.ShapeDtypeStruct((24, LEN), f32),
        in_specs=[pl.BlockSpec(memory_space=pl.ANY)] * 4,
        out_specs=vmem,
        scratch_shapes=[
            pltpu.VMEM((LEN, LEN, LEN), f32),
            pltpu.VMEM((LEN * LEN, 2 * LEN), bf16),
            pltpu.VMEM((LEN * LEN, 2 * LEN), bf16),
            *[pltpu.VMEM(shape, f32) for shape in blocks],
            pltpu.VMEM((2, SR, SR), bf16),
            pltpu.VMEM((2, SR, SR), bf16),
            *[pltpu.VMEM((LEN, SR), f32) for _ in range(6)],
            *[pltpu.VMEM(shape, f32) for shape in blocks],
            *[pltpu.VMEM(shape, f32) for shape in blocks],
            *[pltpu.VMEM(shape, f32) for shape in parts],
            *[pltpu.VMEM(shape, f32) for shape in parts],
            pltpu.SemaphoreType.DMA((CHUNKS,)),
            pltpu.SemaphoreType.DMA((3,)),
            pltpu.SemaphoreType.DMA((12,)),
            pltpu.SemaphoreType.DMA((12,)),
        ],
        compiler_params=pltpu.CompilerParams(
            collective_id=0, has_side_effects=True, vmem_limit_bytes=56 * 2**20
        ),
    )(tensor, factor_a, factor_b, factor_c)
    if not True:
        return packed[0:8], packed[16:20], packed[8:16]
    return pl.pallas_call(
        unpack,
        out_shape=[jax.ShapeDtypeStruct(v.shape, f32) for v in (factor_a, factor_b, factor_c)],
        in_specs=[vmem],
        out_specs=[vmem, vmem, vmem],
    )(packed)


def solution(mesh):
    in_specs = (
        P("gx", "gy", "gz"),
        P(("gy", "gz"), "gx"),
        P(("gx", "gz"), "gy"),
        P(("gx", "gy"), "gz"),
    )
    out_specs = (P(("gy", "gz"), "gx"), P(("gx", "gz"), "gy"), P(("gx", "gy"), "gz"))
    return jax.shard_map(body, mesh=mesh, in_specs=in_specs, out_specs=out_specs, check_vma=False)
```

time: 1200 us -> 39.6 us (0.03); the launches traced: 1190 us -> 39.4 us
  waiting for transfers between devices: 798 us -> 0 us
  blocking collectives: 181 us -> 0 us
  matrix products: 162 us -> 0 us
  Pallas kernels: 0 us -> 38.8 us
  local copies, waits for them, and re-layouts: 23.6 us -> 0 us
  between operations: 16.7 us -> 0.64 us
    unnamed x9 -> x0, waiting for transfers between devices: 798 us -> none
    all_gather x3 -> x0, blocking collectives: 181 us -> none  [the longest x1 84.6 us: body(): block_b = lax.all_gather(factor_b, ('gx', 'gz'), axis=0, tiled=True)]
    dot_general x26 -> x0, matrix products: 162 us -> none  [the longest x4 42.8 us: mode_two(): second_y = jnp.einsum('ijk,ck->cij', tensor, part_c, precision=exact_mode)]
    pallas_call x0 -> x2, Pallas kernels: none -> 38.8 us  [the longest x1 37.5 us: body(): pl.pallas_call(kernel, out_shape=jax.ShapeDtypeStruct((24, LEN), f32), in...]
    dot_general x4 -> x0, local copies, waits for them, and re-layouts: 21.8 us -> none  [mode_one(): first_y = jnp.einsum('ijk,cj->cik', tensor, part_b, precision=exact_mode)]
  transfers between devices with their start and end apart: 6 -> 0, of which waited for: 3 -> 0; matrix products, arithmetic and copies ran while one was open for 16% -> 0% of each run, Pallas kernels for 0% -> 0%
where the time goes in v2:
time: 39.6 us; the launch traced here: 39.4 us
  Pallas kernels  38.8 us (98%)
  between operations  0.64 us (2%)
    pallas_call x1, Pallas kernels, body(): pl.pallas_call(kernel, out_shape=jax.ShapeDtypeStruct((24, LEN), f32), in...  37.5 us
    pallas_call x1, Pallas kernels, body(): pl.pallas_call(unpack, out_shape=[jax.ShapeDtypeStruct(v.shape, f32) for...  1.31 us

profile of v2, /device:TPU:1, one launch (start us, length us, event | category | flops | bytes accessed | tf_op | source)
XLA Modules:
  0.0 39.4 jit_solution(2223989695375581450)
XLA Ops:
  0.6 37.5 %shard_map.67.packed = f32[24,128]{1,0:T(8,128)} custom-call(f32[128,128,128]{2,1,0:T(8,128)} %t_hbm.1, f32[8,128]{1,0:T(8,128)} %a_in.1, f32[4,128]{1,0:T(4,128)} %b_in.1, f32[8,128]{1,0:T(8,128)} %c_in.1), custom_call_target="tpu_custom_call" | custom-call | tf_op jit(solution)/shard_map/pallas_call | solution.py:340
  38.1 1.3 %shard_map.68 = (f32[8,128]{1,0:T(8,128)}, f32[4,128]{1,0:T(4,128)}, f32[8,128]{1,0:T(8,128)}) custom-call(f32[24,128]{1,0:T(8,128)} %shard_map.67.packed), custom_call_target="tpu_custom_call" | custom-call | tf_op jit(solution)/shard_map/pallas_call | solution.py:368

commit v3 on v0

v3 whole, which is shorter than its diff:
```python
import jax
import jax.numpy as jnp
from jax import lax
from jax.experimental import pallas as pl
from jax.experimental.pallas import tpu as pltpu
from jax.sharding import PartitionSpec as P

R = 64
SR = 256
LEN = 128
CHUNKS = 8
STEP = 64
MESH = pl.DeviceIdType.MESH
bf16 = jnp.bfloat16
f32 = jnp.float32


def split(value):
    high = value.astype(bf16)
    return high, (value - high.astype(f32)).astype(bf16)


def stacked(value):
    high, low = split(value)
    return jnp.concatenate([high, high], 0), jnp.concatenate([low, low], 0)


def mm(left, right):
    return jnp.dot(left, right, preferred_element_type=f32)


def offsets(zh=1, zl=1, y=1, x=1, core=1):
    found = [
        (a, b, c, d, e)
        for a in range(zh) for b in range(zl) for c in range(y) for d in range(x) for e in range(core)
    ]

    def hops(o):
        return min(2 * o[0], 8 - 2 * o[0]) + o[1] + min(o[2], 4 - o[2]) + min(o[3], 4 - o[3]) + o[4] * 0.1

    return sorted(found, key=hops, reverse=True)[:-1]


def kernel(
    t_hbm, a_in, b_in, c_in, out,
    t_in, x_rows, x_cols, wb, wc, a_t, c_t, m_a, acc_a, acc_b, acc_c,
    ga, gb, gc, pa, pb, pc, ra, rb, rc, sa, sc, qa, qc,
    t_sem, in_sem, send, recv,
):
    gx, gy, gz = lax.axis_index("gx"), lax.axis_index("gy"), lax.axis_index("gz")
    z_lo, y = gx // 4, gx % 4
    x, core = gz // 2, gz % 2
    me = (gx, gy, gz)

    def peer_of(o):
        a, b, c, d, e = o
        return ((z_lo + b) % 2) * 4 + (y + c) % 4, (gy + a) % 4, ((x + d) % 4) * 2 + (core + e) % 2

    def put(src, dst, peer, stage):
        pltpu.make_async_remote_copy(
            src_ref=src, dst_ref=dst, send_sem=send.at[stage], recv_sem=recv.at[stage],
            device_id=peer, device_id_type=MESH,
        ).start()

    def wait_bytes(ref, sem):
        pltpu.make_async_copy(ref, ref, sem).wait()

    started = []

    def arrived(ref, stage):
        wait_bytes(ref, recv.at[stage])
        started.append((ref, stage))

    def at_x(d, e):
        return ((x + d) % 4) * 2 + (core + e) % 2

    gz_peers = [(gx, gy, at_x(d, e)) for d, e in ((2, 1), (2, 0), (1, 1), (3, 1), (1, 0), (3, 0), (0, 1))]
    y_peers = [(z_lo * 4 + (y + c) % 4, gy, gz) for c in (2, 1, 3)]
    a_far = [(gx, (gy + 2) % 4, gz)]
    a_near = [(gx, (gy + a) % 4, gz) for a in (1, 3)]

    def at_z(a, b):
        if b == 0:
            return gx, (gy + a) % 4, gz
        return (1 - z_lo) * 4 + y, (gy + a * (1 - 2 * z_lo) + 8) % 4, gz

    c_far = [at_z(2, 0), at_z(1, 1), at_z(2, 1)]
    c_near = [at_z(1, 0), at_z(3, 0), at_z(0, 1), at_z(3, 1)]
    b_first = [peer_of(o) for o in offsets(zl=2, y=4)]
    b_full = [peer_of(o) for o in offsets(zl=2, y=4, x=4, core=2)]
    partners = a_far + [at_z(2, 1), at_z(1, 1)] + a_near + [at_z(3, 1)] + b_full

    def block_a(ref, d):
        return ref.at[d[1], d[2]]

    def block_b(ref, d):
        return ref.at[d[0], d[2]]

    def block_c(ref, d):
        return ref.at[d[0] // 4, d[0] % 4, d[1]]

    def send_block(block, ref, device, peers, stage):
        for peer in peers:
            put(block(ref, device), block(ref, device), peer, stage)

    per = LEN // CHUNKS

    def t_copy(n):
        rows = pl.ds(n * per, per)
        return pltpu.make_async_copy(t_hbm.at[rows], t_in.at[rows], t_sem.at[n])

    barrier = pltpu.get_barrier_semaphore()
    for peer in partners:
        pl.semaphore_signal(barrier, inc=1, device_id=peer, device_id_type=MESH)
    own = [
        pltpu.make_async_copy(src, dst, in_sem.at[n])
        for n, (src, dst) in enumerate(((a_in, block_a(ga, me)), (b_in, block_b(gb, me)), (c_in, block_c(gc, me))))
    ]
    for copy in own:
        copy.start()
    for n in range(CHUNKS):
        t_copy(n).start()
    for copy in own:
        copy.wait()
    pl.semaphore_wait(barrier, len(partners))

    send_block(block_c, gc, me, c_far, 0)
    send_block(block_a, ga, me, a_far, 2)
    send_block(block_c, gc, me, c_near, 1)
    send_block(block_a, ga, me, a_near, 3)
    send_block(block_b, gb, me, b_first, 4)
    send_block(block_c, gc, me, y_peers, 5)
    send_block(block_a, ga, me, gz_peers, 6)

    def prepare(first, last):
        for n in range(first, last):
            t_copy(n).wait()

            def body(it, _):
                for u in range(4):
                    i = n * per + it * 4 + u
                    rows = pl.ds(pl.multiple_of(i * LEN, LEN), LEN)
                    value = t_in[i]
                    high, low = split(value)
                    x_rows[rows, 0:LEN] = high
                    x_rows[rows, LEN:] = low
                    high, low = split(value.T)
                    x_cols[rows, 0:LEN] = high
                    x_cols[rows, LEN:] = low
                return 0

            lax.fori_loop(0, per // 4, body, 0)

    prepare(0, 5)
    arrived(sc.at[0:4], 1)
    for device in c_near:
        send_block(block_c, gc, device, y_peers, 5)
    arrived(sa.at[0:2], 3)
    for device in a_near:
        send_block(block_a, ga, device, gz_peers, 6)
    prepare(5, 6)
    arrived(gb.at[0, 0:7], 4)
    for peer in gz_peers:
        put(gb.at[:, gz], gb.at[:, gz], peer, 7)
    prepare(6, 7)
    arrived(sc.at[0:3], 0)
    for device in c_far:
        send_block(block_c, gc, device, y_peers, 5)
    arrived(sa.at[0:1], 2)
    for device in a_far:
        send_block(block_a, ga, device, gz_peers, 6)
    prepare(7, 8)

    def gram(rows, weights):
        left = jnp.concatenate(split(rows), 1)
        return mm(left, weights[0]) + mm(left, weights[1])

    def hess(left, right):
        mask = (
            lax.broadcasted_iota(jnp.int32, (SR, SR), 0) // R
            == lax.broadcasted_iota(jnp.int32, (SR, SR), 1) // R
        )
        return split(jnp.where(mask, left * right, 0.0))

    def hess_term(cols, hessian):
        high, low = hessian
        cols_high, cols_low = split(cols)
        return mm(cols_high, high) + mm(cols_low, high) + mm(cols_high, low)

    arrived(gb.at[0:7], 7)
    rows_b = gb[...].reshape(SR, LEN)
    cols_b = rows_b.T
    weights_b = stacked(cols_b)
    wb[0], wb[1] = weights_b
    gram_b = gram(rows_b, weights_b)
    arrived(ra.at[0:7], 6)
    rows_a = ga[...].reshape(SR, LEN)
    cols_a = rows_a.T
    a_t[...] = cols_a
    gram_a = gram(rows_a, stacked(cols_a))
    hess_c = hess(gram_a, gram_b)
    arrived(rc.at[0:3], 5)
    rows_c = gc[...].reshape(SR, LEN)
    cols_c = rows_c.T
    c_t[...] = cols_c
    weights_c = stacked(cols_c)
    wc[0], wc[1] = weights_c
    gram_c = gram(rows_c, weights_c)
    acc_a[...] = hess_term(cols_a, hess(gram_b, gram_c))
    acc_b[...] = hess_term(cols_b, hess(gram_a, gram_c))
    acc_c[...] = hess_term(cols_c, hess_c)

    def product(x, w, it):
        rows = x[pl.ds(pl.multiple_of(it * (STEP * LEN), STEP * LEN), STEP * LEN), :]
        return (mm(rows, w[0]) + mm(rows, w[1])).reshape(STEP, LEN, SR)

    def cols_step(it, _):
        value = product(x_cols, wb, it)
        total = acc_c[...]
        other = c_t[...]
        for u in range(STEP):
            i = pl.ds(it * STEP + u, 1)
            total = total - value[u] * a_t[i, :]
            m_a[i, :] = jnp.sum(value[u] * other, axis=0, keepdims=True)
        acc_c[...] = total
        return 0

    lax.fori_loop(0, LEN // STEP, cols_step, 0)

    def slot_c(d):
        return d[0] // 4 * 4 + d[1]

    pc[...] = acc_c[...].T.reshape(pc.shape)
    for peer in y_peers:
        put(pc.at[:, peer[0] % 4], rc.at[y], peer, 8)
    pa[...] = (acc_a[...] - m_a[...]).T.reshape(pa.shape)
    for peer in gz_peers:
        put(pa.at[:, peer[2]], ra.at[gz], peer, 9)

    def rows_step(it, _):
        value = product(x_rows, wc, it)
        total = acc_b[...]
        for u in range(STEP):
            total = total - value[u] * a_t[pl.ds(it * STEP + u, 1), :]
        acc_b[...] = total
        return 0

    lax.fori_loop(0, LEN // STEP, rows_step, 0)

    pb[...] = acc_b[...].T.reshape(pb.shape)
    for peer in b_full:
        put(block_b(pb, peer), rb.at[gx * 8 + gz], peer, 10)
    arrived(rc.at[0:3], 8)
    rc[y] = pc[:, y]
    sc[...] = ((rc[0] + rc[1]) + (rc[2] + rc[3])).reshape(sc.shape)
    for peer in c_far + c_near:
        put(sc.at[slot_c(peer)], qc.at[slot_c(me)], peer, 11)
    arrived(ra.at[0:7], 9)
    ra[gz] = pa[:, gz]
    sa[...] = ((ra[0] + ra[1]) + (ra[2] + ra[3])) + ((ra[4] + ra[5]) + (ra[6] + ra[7]))
    for peer in a_far + a_near:
        put(sa.at[peer[1]], qa.at[gy], peer, 12)
    arrived(sc.at[0:7], 11)
    qc[slot_c(me)] = sc[slot_c(me)]
    out[8:16] = jnp.sum(qc[...], axis=0)
    arrived(sa.at[0:3], 12)
    qa[gy] = sa[gy]
    out[0:8] = (qa[0] + qa[1]) + (qa[2] + qa[3])
    arrived(rb.at[0:63], 10)
    rb[gx * 8 + gz] = pb[gx, gz]
    out[16:20] = jnp.sum(rb[...], axis=0)

    for ref, stage in started:
        wait_bytes(ref, send.at[stage])


def unpack(packed, a_out, b_out, c_out):
    a_out[...] = packed[0:8]
    c_out[...] = packed[8:16]
    b_out[...] = packed[16:20]


def body(tensor, factor_a, factor_b, factor_c):
    vmem = pl.BlockSpec(memory_space=pltpu.VMEM)
    blocks = [(4, 8, 8, LEN), (8, 8, 4, LEN), (2, 4, 4, 8, LEN)]
    slots = [(8, 4, 8, LEN), (64, 4, LEN), (4, 2, 4, 8, LEN)]
    parts = [(4, 8, LEN), (8, 8, LEN)]
    packed = pl.pallas_call(
        kernel,
        out_shape=jax.ShapeDtypeStruct((24, LEN), f32),
        in_specs=[pl.BlockSpec(memory_space=pl.ANY)] * 4,
        out_specs=vmem,
        scratch_shapes=[
            pltpu.VMEM((LEN, LEN, LEN), f32),
            pltpu.VMEM((LEN * LEN, 2 * LEN), bf16),
            pltpu.VMEM((LEN * LEN, 2 * LEN), bf16),
            pltpu.VMEM((2, SR, SR), bf16),
            pltpu.VMEM((2, SR, SR), bf16),
            *[pltpu.VMEM((LEN, SR), f32) for _ in range(6)],
            *[pltpu.VMEM(shape, f32) for shape in blocks + blocks + slots + parts + parts],
            pltpu.SemaphoreType.DMA((CHUNKS,)),
            pltpu.SemaphoreType.DMA((3,)),
            pltpu.SemaphoreType.DMA((13,)),
            pltpu.SemaphoreType.DMA((13,)),
        ],
        compiler_params=pltpu.CompilerParams(
            collective_id=0, has_side_effects=True, vmem_limit_bytes=56 * 2**20
        ),
    )(tensor, factor_a, factor_b, factor_c)
    if not True:
        return packed[0:8], packed[16:20], packed[8:16]
    return pl.pallas_call(
        unpack,
        out_shape=[jax.ShapeDtypeStruct(v.shape, f32) for v in (factor_a, factor_b, factor_c)],
        in_specs=[vmem],
        out_specs=[vmem, vmem, vmem],
    )(packed)


def solution(mesh):
    in_specs = (
        P("gx", "gy", "gz"),
        P(("gy", "gz"), "gx"),
        P(("gx", "gz"), "gy"),
        P(("gx", "gy"), "gz"),
    )
    out_specs = (P(("gy", "gz"), "gx"), P(("gx", "gz"), "gy"), P(("gx", "gy"), "gz"))
    return jax.shard_map(body, mesh=mesh, in_specs=in_specs, out_specs=out_specs, check_vma=False)
```

time: 1200 us -> 39.3 us (0.03); the launches traced: 1190 us -> 39.1 us
  waiting for transfers between devices: 798 us -> 0 us
  blocking collectives: 181 us -> 0 us
  matrix products: 162 us -> 0 us
  Pallas kernels: 0 us -> 38.5 us
  local copies, waits for them, and re-layouts: 23.6 us -> 0 us
  between operations: 16.7 us -> 0.64 us
    unnamed x9 -> x0, waiting for transfers between devices: 798 us -> none
    all_gather x3 -> x0, blocking collectives: 181 us -> none  [the longest x1 84.6 us: body(): block_b = lax.all_gather(factor_b, ('gx', 'gz'), axis=0, tiled=True)]
    dot_general x26 -> x0, matrix products: 162 us -> none  [the longest x4 42.8 us: mode_two(): second_y = jnp.einsum('ijk,ck->cij', tensor, part_c, precision=exact_mode)]
    pallas_call x0 -> x2, Pallas kernels: none -> 38.5 us  [the longest x1 37.2 us: body(): pl.pallas_call(kernel, out_shape=jax.ShapeDtypeStruct((24, LEN), f32), in...]
    dot_general x4 -> x0, local copies, waits for them, and re-layouts: 21.8 us -> none  [mode_one(): first_y = jnp.einsum('ijk,cj->cik', tensor, part_b, precision=exact_mode)]
  transfers between devices with their start and end apart: 6 -> 0, of which waited for: 3 -> 0; matrix products, arithmetic and copies ran while one was open for 16% -> 0% of each run, Pallas kernels for 0% -> 0%
where the time goes in v3:
time: 39.3 us; the launch traced here: 39.1 us
  Pallas kernels  38.5 us (98%)
  between operations  0.64 us (2%)
    pallas_call x1, Pallas kernels, body(): pl.pallas_call(kernel, out_shape=jax.ShapeDtypeStruct((24, LEN), f32), in...  37.2 us
    pallas_call x1, Pallas kernels, body(): pl.pallas_call(unpack, out_shape=[jax.ShapeDtypeStruct(v.shape, f32) for...  1.31 us

profile of v3, /device:TPU:1, one launch (start us, length us, event | category | flops | bytes accessed | tf_op | source)
XLA Modules:
  0.0 39.1 jit_solution(15095013651219765233)
XLA Ops:
  0.6 37.2 %shard_map.67.packed = f32[24,128]{1,0:T(8,128)} custom-call(f32[128,128,128]{2,1,0:T(8,128)} %t_hbm.1, f32[8,128]{1,0:T(8,128)} %a_in.1, f32[4,128]{1,0:T(4,128)} %b_in.1, f32[8,128]{1,0:T(8,128)} %c_in.1), custom_call_target="tpu_custom_call" | custom-call | tf_op jit(solution)/shard_map/pallas_call | solution.py:288
  37.8 1.3 %shard_map.68 = (f32[8,128]{1,0:T(8,128)}, f32[4,128]{1,0:T(4,128)}, f32[8,128]{1,0:T(8,128)}) custom-call(f32[24,128]{1,0:T(8,128)} %shard_map.67.packed), custom_call_target="tpu_custom_call" | custom-call | tf_op jit(solution)/shard_map/pallas_call | solution.py:312

commit v4 on v3

--- a/solution.py
+++ b/solution.py
@@ -247,9 +247,6 @@
 
     lax.fori_loop(0, LEN // STEP, rows_step, 0)
 
-    pb[...] = acc_b[...].T.reshape(pb.shape)
-    for peer in b_full:
-        put(block_b(pb, peer), rb.at[gx * 8 + gz], peer, 10)
     arrived(rc.at[0:3], 8)
     rc[y] = pc[:, y]
     sc[...] = ((rc[0] + rc[1]) + (rc[2] + rc[3])).reshape(sc.shape)
@@ -260,6 +257,9 @@
     sa[...] = ((ra[0] + ra[1]) + (ra[2] + ra[3])) + ((ra[4] + ra[5]) + (ra[6] + ra[7]))
     for peer in a_far + a_near:
         put(sa.at[peer[1]], qa.at[gy], peer, 12)
+    pb[...] = acc_b[...].T.reshape(pb.shape)
+    for peer in b_full:
+        put(block_b(pb, peer), rb.at[gx * 8 + gz], peer, 10)
     arrived(sc.at[0:7], 11)
     qc[slot_c(me)] = sc[slot_c(me)]
     out[8:16] = jnp.sum(qc[...], axis=0)

time: 39.3 us -> 39.9 us (1.015)
  Pallas kernels: 38.5 us -> 39.1 us
    pallas_call x1, Pallas kernels: 37.2 us -> 37.8 us  [body(): pl.pallas_call(kernel, out_shape=jax.ShapeDtypeStruct((24, LEN), f32), in...]
where the time goes in v4:
time: 39.9 us; the launch traced here: 39.7 us
  Pallas kernels  39.1 us (98%)
  between operations  0.64 us (2%)
    pallas_call x1, Pallas kernels, body(): pl.pallas_call(kernel, out_shape=jax.ShapeDtypeStruct((24, LEN), f32), in...  37.8 us
    pallas_call x1, Pallas kernels, body(): pl.pallas_call(unpack, out_shape=[jax.ShapeDtypeStruct(v.shape, f32) for...  1.31 us

profile of v4, /device:TPU:1, one launch (start us, length us, event | category | flops | bytes accessed | tf_op | source)
XLA Modules:
  0.0 39.7 jit_solution(11670599485828408208)
XLA Ops:
  0.6 37.8 %shard_map.67.packed = f32[24,128]{1,0:T(8,128)} custom-call(f32[128,128,128]{2,1,0:T(8,128)} %t_hbm.1, f32[8,128]{1,0:T(8,128)} %a_in.1, f32[4,128]{1,0:T(4,128)} %b_in.1, f32[8,128]{1,0:T(8,128)} %c_in.1), custom_call_target="tpu_custom_call" | custom-call | tf_op jit(solution)/shard_map/pallas_call | solution.py:288
  38.4 1.3 %shard_map.68 = (f32[8,128]{1,0:T(8,128)}, f32[4,128]{1,0:T(4,128)}, f32[8,128]{1,0:T(8,128)}) custom-call(f32[24,128]{1,0:T(8,128)} %shard_map.67.packed), custom_call_target="tpu_custom_call" | custom-call | tf_op jit(solution)/shard_map/pallas_call | solution.py:312
